TPU v7x, 32 devices: a whole 2x2x4 slice. The times are simulated.
32 devices in a mesh: areal: 16 (over z, y, x), layer: 2 (over core).
Axes of the slice: x: 2, y: 2, z: 4, core: 2. Of those that a mesh axis runs over, the one named last changes fastest.
Arguments:
- rhs: bfloat16 [16, 4, 112, 384], P('areal', 'layer'), may hold values from -6 to 6
- areal_blocks: bfloat16 [16, 4, 6, 384, 384], P('areal', 'layer'), may hold values from -0.078125 to 0.078125
- vertical_blocks: bfloat16 [16, 4, 2, 384, 384], P('areal', 'layer'), may hold values from -0.078125 to 0.078125
- conn_src: int32 [16, 2, 6], P('areal', 'layer'), may hold values from 0 to 31, as said below
- conn_count: int32 [16, 2], P('areal', 'layer'), may hold values from 1 to 6, as said below
- tile_map: int32 [32], replicated, may hold values from 0 to 31, as said below
- well_cells: int32 [16, 4, 4], P('areal', 'layer'), may hold values from 0 to 127
- well_gain: float32 [16, 4, 4], P('areal', 'layer'), may hold values from -24 to 24
- sens: float32 [16, 4, 3, 128], P('areal', 'layer'), may hold values from -6 to 6
- basis: bfloat16 [16, 4, 128, 256], P('areal', 'layer'), may hold values from -0.0625 to 0.0625
Outputs:
- adjoint: bfloat16 [16, 4, 112, 384], P('areal', 'layer')
- coefficients: bfloat16 [112, 256], P('layer', 'areal')
Inputs may be any that keep to these rules, and one draw needn't show every extreme that they name: Tile t of a layer group's plane is held by device column tile_map[t] // 2 in tile layer 2 g + tile_map[t] % 2; each value is held by one tile. `conn_src`: the 6 sources of device column c lie, in some order, on the 6 device columns (c + k) mod 16 with k one of 1 to 2, their negatives, 8 and 9, one on each. `conn_count`: the live connections of a device are its first ones. `well_cells`: cells of a tile, repeats allowed.
All inputs are finite; a program needn't handle non-finite values.
Results may differ from a plain program's by a relative error of at most 0.02.
Values may be sent and summed in bfloat16 or wider, within the bound.
No kernel may reach another device: no remote copies, remote signals or barrier semaphores. Data moves between devices by JAX's collectives and lax.ppermute only.
A program may use at most 64 MiB of HBM per device.

v0:
```python
import functools

import jax
import jax.numpy as jnp
from jax import lax
from jax.experimental import pallas as pl
from jax.experimental.pallas import tpu as pltpu
from jax.sharding import PartitionSpec as P

ITERS = 3
F32 = jnp.float32
BF16 = jnp.bfloat16
SMEM = pl.BlockSpec(memory_space=pltpu.SMEM)
VMEM = pl.BlockSpec(memory_space=pltpu.VMEM)
LIMIT = 16 * 1024 * 1024


def near_swaps(count):
    return [(k, color) for color in (1, 0) for k in range(count // 2 - 1, 0, -1)]


def swap_pairs(columns, k, color):
    return [
        (c, (c + k if (c // k) % 2 == color else c - k) % columns) for c in range(columns)
    ]


def held(x):
    return pltpu.with_memory_space_constraint(x, pltpu.VMEM)


def dot(a, b):
    return jnp.dot(a, b, preferred_element_type=F32)


def plan_kernel(columns, swaps, src, count, tile_map, me, group, rhs, table, asks, payload):
    steps = [
        jnp.where(lax.rem(lax.div(me[0], k), 2) == color, k, columns - k) for k, color in swaps
    ] + [columns // 2 + 1, columns // 2]
    number = len(steps)
    conn = [0] * number
    slots = [0] * number
    for s in range(number):
        place = tile_map[src[s]]
        peer = lax.shift_right_logical(place, 1)
        slot = lax.bitwise_and(place, 1)
        away = peer - me[0]
        away = jnp.where(away < 0, away + columns, away)
        for i, k in enumerate(steps):
            hit = away == k
            conn[i] = jnp.where(hit, s, conn[i])
            slots[i] = jnp.where(hit, slot, slots[i])
    line = lax.broadcasted_iota(jnp.int32, asks.shape, 0)
    asked = jnp.zeros(line.shape, F32)
    for i in range(number):
        table[i] = conn[i]
        table[number + i] = jnp.where(conn[i] < count[0], 1, 0)
        asked = jnp.where(line == i, slots[i].astype(F32), asked)
    asked = jnp.where(line == number, group[0].astype(F32), asked)
    asked = jnp.where(line == number + 1, lax.rem(me[0], 2).astype(F32), asked)
    asks[...] = asked
    rows, width = rhs.shape
    payload[0:rows] = rhs[...]
    payload[rows:] = jnp.zeros((16, width), BF16)
    none = jnp.zeros(asked.shape, F32)
    payload[rows:, 0:128] = jnp.concatenate([asked, none], axis=0).astype(BF16)


def load_kernel(number, two, table, group, blocks, vert, bands, sides, sems):
    width = vert.shape[-1]
    mine = group[0]
    ends = [(1 - mine, 1 - mine)] if two else [(0, 0), (1, 1)]
    beside = [
        pltpu.make_async_copy(vert.at[d, k], sides.at[i], sems.at[2 * number + i])
        for i, (d, k) in enumerate([(0, 1), (1, 0), *ends])
    ]
    for copy in beside:
        copy.start()

    def copies(i):
        return [
            pltpu.make_async_copy(
                blocks.at[d, table[i]],
                bands.at[i, :, pl.ds(d * width, width)],
                sems.at[2 * i + d],
            )
            for d in range(2)
        ]

    for i in range(number):

        @pl.when(table[number + i] > 0)
        def _():
            for copy in copies(i):
                copy.start()

        @pl.when(table[number + i] == 0)
        def _():
            bands[i] = jnp.zeros(bands.shape[1:], bands.dtype)

    for i in range(number):

        @pl.when(table[number + i] > 0)
        def _():
            for copy in copies(i):
                copy.wait()

    for copy in beside:
        copy.wait()


def turn_kernel(columns, basis, turned):
    _, cells, modes = basis.shape
    bands = []
    for d in range(2):
        by_mode = basis[d].astype(F32).T.reshape(columns, 2, modes // columns // 2, cells)
        bands += [by_mode[:, h].reshape(modes // 2, cells) for h in range(2)]
    turned[...] = jnp.concatenate(bands, axis=1).astype(BF16)


def weigh_kernel(wells, gains, sens, factors):
    cells = sens.shape[-1]
    spot = lax.broadcasted_iota(jnp.int32, (1, cells), 1)
    factors[...] = sens[...]
    for d in range(2):
        well = jnp.zeros((1, cells), F32)
        for w in range(wells.shape[1]):
            well = well + jnp.where(spot == wells[d, w], gains[d, w], 0.0)
        factors[0, d : d + 1, :] = sens[0, d : d + 1, :] + well


def wide(mask, width):
    return jnp.concatenate([mask] * (width // mask.shape[1]), axis=1)


def chosen(mask, low, high):
    return jnp.where(wide(mask, low.shape[1]) > 0.5, high, low).astype(BF16)


def asks_of(payload):
    return payload[payload.shape[0] - 16 :, 0:128].astype(F32)


def tile_of(ref, mask, rows):
    if ref.shape[0] == rows:
        return ref[...]
    return chosen(mask, ref[0:rows].astype(F32), ref[rows : 2 * rows].astype(F32))


def cross_pick_kernel(lines, me, tile_map, *refs):
    count = len(lines)
    tables, payload, known, tiles = refs[:count], refs[count], refs[count + 1], refs[count + 2 :]
    rows = tiles[0].shape[0]
    line = lax.broadcasted_iota(jnp.int32, known.shape, 0)
    masks = jnp.zeros(known.shape, F32)
    for i, table in zip(lines, tables):
        wanted = 0
        for s in range(table.shape[-1]):
            place = tile_map[table[s]]
            peer = lax.shift_right_logical(place, 1)
            wanted = jnp.where(peer == me[0], lax.bitwise_and(place, 1), wanted)
        masks = jnp.where(line == i, wanted.astype(F32), masks)
    known[...] = masks
    low, high = payload[0:rows].astype(F32), payload[rows : 2 * rows].astype(F32)
    for i, tile in zip(lines, tiles):
        tile[...] = chosen(masks[i : i + 1, :], low, high)


def own_kernel(lam, rhs, sides, part):
    rows = rhs.shape[0] // 2
    part[0] = rhs[0:rows].astype(F32) - dot(lam[rows : 2 * rows], sides[0])
    part[1] = rhs[rows:].astype(F32) - dot(lam[0:rows], sides[1])


def source_sums(asks, bands, begin, refs, rows):
    tiles = [tile_of(ref, asks[i : i + 1, :], rows) for i, ref in enumerate(refs, begin)]
    count, width, both = len(refs), bands.shape[1], bands.shape[2]
    band = bands[begin : begin + count].reshape(count * width, both)
    sums = dot(jnp.concatenate(tiles, axis=1), band)
    return sums[:, :width], sums[:, width:]


def beside_sums(number, two, asks, sides, beside, rows):
    if two:
        mine = asks[number : number + 1, :]
        term = dot(tile_of(beside[0], mine, rows), sides[2])
        above = wide(mine, term.shape[1]) > 0.5
        none = jnp.zeros_like(term)
        return jnp.where(above, term, none), jnp.where(above, none, term)
    return [
        dot(tile_of(beside[d], jnp.full((1, 128), 1.0 - d, F32), rows), sides[2 + d])
        for d in range(2)
    ]


def cross_kernel(asks, bands, *refs):
    arrived, out = refs[:-1], refs[-1]
    out[0], out[1] = source_sums(asks, bands, 0, arrived, out.shape[1])


def far_kernel(asks, bands, cross, *refs):
    far, out = refs[:-1], refs[-1]
    low, high = source_sums(asks, bands, bands.shape[0] - len(far), far, out.shape[1])
    out[0] = cross[0] + low
    out[1] = cross[1] + high


def local_kernel(number, two, begin, asks, bands, sides, *refs):
    here = number - 2 - begin
    near, beside, out = refs[:here], refs[here:-1], refs[-1]
    rows = out.shape[1]
    sums = source_sums(asks, bands, begin, near, rows)
    terms = beside_sums(number, two, asks, sides, beside, rows)
    for d in range(2):
        out[d] = sums[d] + terms[d]


def updated(number, two, begin, part, far, asks, bands, sides, near, beside):
    rows = part.shape[1]
    sums = source_sums(asks, bands, begin, near, rows)
    terms = beside_sums(number, two, asks, sides, beside, rows)
    return [part[d] - far[d] - sums[d] - terms[d] for d in range(2)]


def update_kernel(number, two, begin, first, part, far, asks, *refs):
    ends = 1 if two else 2
    here = number - 2 - begin
    if first:
        local, refs = refs[0], refs[1:]
        low, high = [part[d] - far[d] - local[d] for d in range(2)]
    else:
        (bands, sides), refs = refs[:2], refs[2:]
        near, refs = refs[:here], refs[here:]
        beside, refs = refs[:ends], refs[ends:]
        low, high = updated(number, two, begin, part, far, asks, bands, sides, near, beside)
    count = 1 + here if first else 1
    told, refs = refs[:count], refs[count:]
    lam, sends, refs = refs[0], refs[1 : 1 + number], refs[1 + number :]
    outer, refs = refs[:ends], refs[ends:]
    masks = told[0]
    if first:
        masks = refs[0]
        masks[...] = told[0][...]
        for i, ref in enumerate(told[1:], begin):
            masks[i : i + 1, :] = asks_of(ref)[i : i + 1, :]
    rows = low.shape[0]
    lam[0:rows] = low.astype(BF16)
    lam[rows:] = high.astype(BF16)
    for i, send in enumerate(sends):
        send[...] = chosen(masks[i : i + 1, :], low, high)
    if two:
        outer[0][...] = chosen(asks[number : number + 1, :], high, low)
    else:
        outer[0][...] = high.astype(BF16)
        outer[1][...] = low.astype(BF16)


def last_kernel(number, two, begin, part, far, asks, bands, sides, factors, basis, *refs):
    here = number - 2 - begin
    near, beside, (lam, pieces) = refs[:here], refs[here:-2], refs[-2:]
    sums = updated(number, two, begin, part, far, asks, bands, sides, near, beside)
    phases, _, cells = factors.shape
    grads = []
    for d in range(2):
        rounded = sums[d].astype(BF16)
        lam[d] = rounded
        back = rounded.astype(F32)
        grad = back[:, :cells] * factors[0, d : d + 1, :]
        for p in range(1, phases):
            grad = grad + back[:, p * cells : (p + 1) * cells] * factors[p, d : d + 1, :]
        grads.append(grad)
    if two:
        half = grads[0].shape[0] // 2
        none = jnp.zeros((half, cells), F32)
        band = pieces.shape[1]
        for g in range(2):
            cuts = [grad[g * half : (g + 1) * half] for grad in grads]
            top = jnp.concatenate([x for cut in cuts for x in (cut, none)], axis=1)
            low = jnp.concatenate([x for cut in cuts for x in (none, cut)], axis=1)
            wing = jnp.concatenate([top, low], axis=0).astype(BF16)
            share = lax.dot_general(
                basis[...], wing, (((1,), (1,)), ((), ())), preferred_element_type=F32
            )
            for c in range(pieces.shape[0] // 2):
                pieces[2 * c + g] = share[c * band : (c + 1) * band].astype(BF16)
    else:
        terms = [dot(grad.astype(BF16), basis[d]) for d, grad in enumerate(grads)]
        pieces[...] = terms[0] + terms[1]


def sum_kernel(pieces, out):
    total = pieces[0].astype(F32)
    for i in range(1, pieces.shape[0]):
        total = total + pieces[i].astype(F32)
    half = total.shape[1] // 2
    out[...] = jnp.concatenate([total[:, :half], total[:, half:]], axis=0).astype(BF16)


def call(kernel, outs, ins, specs, scratch=(), flops=0, moved=0, out_specs=None):
    return pl.pallas_call(
        kernel,
        out_shape=outs,
        in_specs=specs,
        out_specs=out_specs or [VMEM] * len(outs),
        scratch_shapes=list(scratch),
        compiler_params=pltpu.CompilerParams(vmem_limit_bytes=LIMIT),
        cost_estimate=pl.CostEstimate(
            flops=flops, bytes_accessed=moved or flops // 200, transcendentals=0
        ),
    )(*ins)


def moved_by(x, pairs):
    return held(lax.ppermute(x, "areal", pairs))


def shift_pairs(columns, k):
    return [(i, (i - k) % columns) for i in range(columns)]


def beside_layers(tiles):
    groups = lax.axis_size("layer")
    if groups == 2:
        return [held(lax.ppermute(tiles[0], "layer", [(0, 1), (1, 0)]))]
    up = [(i, i + 1) for i in range(groups - 1)]
    down = [(i + 1, i) for i in range(groups - 1)]
    return [held(lax.ppermute(tiles[0], "layer", up)), held(lax.ppermute(tiles[-1], "layer", down))]


def outside(x):
    return pltpu.with_memory_space_constraint(x, pltpu.HBM)


def on_device(
    rhs,
    areal_blocks,
    vertical_blocks,
    conn_src,
    conn_count,
    tile_map,
    well_cells,
    well_gain,
    sens,
    basis,
):
    columns = lax.axis_size("areal")
    groups = lax.axis_size("layer")
    two = groups == 2
    rows, width = rhs.shape[2:]
    modes = basis.shape[-1]
    number = conn_src.shape[-1]
    swaps = near_swaps(number)
    routes = [swap_pairs(columns, k, color) for k, color in swaps]
    routes += [shift_pairs(columns, columns // 2 + 1), shift_pairs(columns, columns // 2)]
    rhs = rhs[0].reshape(2 * rows, width)
    me = lax.axis_index("areal").astype(jnp.int32).reshape(1)
    group = lax.axis_index("layer").astype(jnp.int32).reshape(1)

    tile = pltpu.VMEM((rows, width), BF16)
    pair = pltpu.VMEM((2 * rows, width), BF16)
    sums = pltpu.VMEM((2, rows, width), F32)
    one = 2 * rows * width * width
    partial = functools.partial

    masks_type = pltpu.VMEM((8, 128), F32)
    with jax.named_scope("plan"):
        half = len(swaps) // 2
        lines = [*range(half), number - 2, number - 1]
        tables = [
            lax.ppermute(conn_src, "areal", [(to, at) for at, to in routes[i]]) for i in lines
        ]
        table, asks, payload = call(
            partial(plan_kernel, columns, swaps),
            [
                jax.ShapeDtypeStruct((2 * number,), jnp.int32),
                masks_type,
                pltpu.VMEM((2 * rows + 16, width), BF16),
            ],
            (outside(conn_src[0, 0]), conn_count[0], outside(tile_map), me, group, outside(rhs)),
            [SMEM] * 5 + [VMEM],
            out_specs=[SMEM] + [VMEM] * 2,
        )
        asks, payload = held(asks), held(payload)
        known, *crossing = call(
            partial(cross_pick_kernel, lines),
            [masks_type] + [tile] * len(lines),
            (me, outside(tile_map), *[x[0, 0] for x in tables], payload),
            [SMEM] * (2 + len(lines)) + [VMEM],
        )
        known = held(known)

    with jax.named_scope("load"):
        bands, sides = call(
            partial(load_kernel, number, two),
            [
                pltpu.VMEM((number, width, 2 * width), BF16),
                pltpu.VMEM((3 if two else 4, width, width), BF16),
            ],
            (table, group, outside(areal_blocks[0]), outside(vertical_blocks[0])),
            [SMEM] * 2 + [pl.BlockSpec(memory_space=pltpu.HBM)] * 2,
            [pltpu.SemaphoreType.DMA((2 * number + 4,))],
            moved=areal_blocks.size * 2 + vertical_blocks.size * 2,
        )
        bands, sides = held(bands), held(sides)
        (factors,) = call(
            weigh_kernel,
            [pltpu.VMEM((sens.shape[2], 2, sens.shape[3]), F32)],
            (well_cells[0], well_gain[0], sens[0].transpose(1, 0, 2)),
            [SMEM] * 2 + [VMEM],
        )
        weights = held(basis[0])
        if two:
            (weights,) = call(
                partial(turn_kernel, columns),
                [pltpu.VMEM((modes // 2, 4 * sens.shape[3]), BF16)],
                (basis[0],),
                [VMEM],
            )
        factors, weights = held(factors), held(weights)

    rhs_held = lam = held(rhs)
    sends = [*crossing[:half], *[payload] * half, *crossing[half:]]
    outer = [payload]
    for step in range(ITERS):
        first = step == 0
        with jax.named_scope("apply"):
            arrived = [moved_by(x, pairs) for x, pairs in zip(sends, routes)]
            (part,) = call(own_kernel, [sums], (lam, rhs_held, sides), [VMEM] * 3, flops=one)
            part = held(part)
            if first:
                told = [known, *arrived[half:-2]]
            beside = beside_layers(outer)
            (cross,) = call(
                cross_kernel,
                [sums],
                (asks, bands, *arrived[:half]),
                [VMEM] * (2 + half),
                flops=4 * one,
            )
            (far,) = call(
                far_kernel,
                [sums],
                (asks, bands, held(cross), *arrived[-2:]),
                [VMEM] * 5,
                flops=(64 if first else 4) * one,
            )
            tiles = (part, held(far), asks, bands, sides)
            near = (*arrived[half:-2], *beside)
            if step < ITERS - 1:
                if first:
                    (local,) = call(
                        partial(local_kernel, number, two, half),
                        [sums],
                        (asks, bands, sides, *near),
                        [VMEM] * (3 + len(near)),
                        flops=96 * one,
                    )
                    given = (part, held(far), asks, held(local))
                else:
                    given = (*tiles, *near)
                lam, *rest = call(
                    partial(update_kernel, number, two, half, first),
                    [pair] + [tile] * (number + len(beside)) + ([masks_type] if first else []),
                    (*given, *told),
                    [VMEM] * (len(given) + len(told)),
                    flops=one,
                )
                lam = held(lam)
                if first:
                    told = [held(rest.pop())]
                sends, outer = rest[:number], rest[number:]
            else:
                adjoint, pieces = call(
                    partial(last_kernel, number, two, half),
                    [
                        jax.ShapeDtypeStruct((2, rows, width), BF16),
                        pltpu.VMEM((2 * columns, modes // columns // 2, rows), BF16)
                        if two
                        else pltpu.VMEM((rows, modes), F32),
                    ],
                    (*tiles, factors, weights, *near),
                    [VMEM] * (7 + len(near)),
                    flops=one,
                )

    with jax.named_scope("project"):
        if two:
            landed = lax.all_to_all(pieces, ("areal", "layer"), 0, 0, tiled=True)
            (coefficients,) = call(
                sum_kernel,
                [jax.ShapeDtypeStruct((modes // columns, rows // 2), BF16)],
                (held(landed),),
                [VMEM],
            )
            coefficients = coefficients.T
        else:
            cut = pieces.reshape(groups, rows // groups, columns, modes // columns)
            cut = cut.transpose(2, 0, 1, 3).reshape(columns * groups, rows // groups, modes // columns)
            landed = lax.all_to_all(cut, ("areal", "layer"), 0, 0, tiled=True)
            coefficients = jnp.sum(landed, axis=0).astype(BF16)
    return (adjoint[None], coefficients)


def solution(mesh):
    in_specs = (
        P("areal", "layer", None, None),
        P("areal", "layer", None, None, None),
        P("areal", "layer", None, None, None),
        P("areal", "layer", None),
        P("areal", "layer"),
        P(),
        P("areal", "layer", None),
        P("areal", "layer", None),
        P("areal", "layer", None, None),
        P("areal", "layer", None, None),
    )
    out_specs = (P("areal", "layer", None, None), P("layer", "areal"))
    return jax.shard_map(
        on_device, mesh=mesh, in_specs=in_specs, out_specs=out_specs, check_vma=False
    )
```

profile of v0, /device:TPU:0, one launch (start us, length us, event | category | flops | bytes accessed | tf_op | source)
XLA Modules:
  0.0 73.5 jit_solution(11450734141986928520)
XLA Ops:
  0.6 4.1 %collective-permute-start.3 = (s32[1,1,6]{2,1,0:T(1,128)}, s32[1,1,6]{2,1,0:T(1,128)S(1)}, u32[]{:S(2)}, u32[]{:S(2)}) collective-permute-start(s32[1,1,6]{2,1,0:T(1,128)} %param.13), channel_id=1, source_target_pairs={{16,0},{18,2},{20,4},{22,6},{24,8},{26,10},{28,12},{30,14},{0,16},... | collective-permute-start | bytes 80 | tf_op jit(solution)/shard_map/plan/ppermute | solution.py:370
  4.7 2.3 %collective-permute-start = (s32[1,1,6]{2,1,0:T(1,128)}, s32[1,1,6]{2,1,0:T(1,128)S(1)}, u32[]{:S(2)}, u32[]{:S(2)}) collective-permute-start(s32[1,1,6]{2,1,0:T(1,128)} %param.13), channel_id=1, source_target_pairs={{28,0},{30,2},{8,4},{10,6},{4,8},{6,10},{16,12},{18,14},{12,16},{1... | collective-permute-start | bytes 80 | tf_op jit(solution)/shard_map/plan/ppermute | solution.py:370
  7.0 3.3 %collective-permute-start.1 = (s32[1,1,6]{2,1,0:T(1,128)}, s32[1,1,6]{2,1,0:T(1,128)S(1)}, u32[]{:S(2)}, u32[]{:S(2)}) collective-permute-start(s32[1,1,6]{2,1,0:T(1,128)} %param.13), channel_id=1, source_target_pairs={{30,0},{4,2},{2,4},{8,6},{6,8},{12,10},{10,12},{16,14},{14,16},{20... | collective-permute-start | bytes 80 | tf_op jit(solution)/shard_map/plan/ppermute | solution.py:370
  11.0 1.6 %plan.2 = (s32[12]{0:T(128)S(1)}, f32[8,128]{1,0:T(8,128)S(1)}, bf16[240,384]{1,0:T(8,128)(2,1)S(1)}) custom-call(s32[6]{0:T(128)} %bitcast.36, s32[1]{0:T(128)} %bitcast.19.count, s32[32]{0:T(128)} %tile_map.3, s32[1]{0:T(128)} %bitcast.3.me, s32[1]{0:T(128)} %bitcast.4.group, bf16[224,384]{1,0:T(8,128)(2,1)} %bitcast.20), custom_call_target="tpu_custom_call" | custom-call | tf_op jit(solution)/shard_map/plan/pallas_call | solution.py:300
  12.7 1.6 %collective-permute-done.1 = s32[1,1,6]{2,1,0:T(1,128)S(1)} collective-permute-done((s32[1,1,6]{2,1,0:T(1,128)}, s32[1,1,6]{2,1,0:T(1,128)S(1)}, u32[]{:S(2)}, u32[]{:S(2)}) %collective-permute-start.1) | collective-permute-done | bytes 56 | tf_op jit(solution)/shard_map/plan/ppermute | solution.py:370
  14.3 1.5 %collective-permute-done.2 = s32[1,1,6]{2,1,0:T(1,128)S(1)} collective-permute-done((s32[1,1,6]{2,1,0:T(1,128)}, s32[1,1,6]{2,1,0:T(1,128)S(1)}, u32[]{:S(2)}, u32[]{:S(2)}) %collective-permute-start.2) | collective-permute-done | bytes 56 | tf_op jit(solution)/shard_map/plan/ppermute | solution.py:370
  17.1 2.8 %collective-permute-start.5 = (bf16[112,384]{1,0:T(8,128)(2,1)S(1)}, bf16[112,384]{1,0:T(8,128)(2,1)S(1)}, u32[]{:S(2)}, u32[]{:S(2)}) collective-permute-start(bf16[112,384]{1,0:T(8,128)(2,1)S(1)} %get-tuple-element.37), channel_id=1, source_target_pairs={{0,30},{2,4},{4,2},{6,8},{8,6},{10,12},{12,10},{14,16},{16,14},{18... | collective-permute-start | bytes 258056 | tf_op jit(solution)/shard_map/apply/ppermute | solution.py:314
  19.9 1.3 %collective-permute-start.6 = (bf16[112,384]{1,0:T(8,128)(2,1)S(1)}, bf16[112,384]{1,0:T(8,128)(2,1)S(1)}, u32[]{:S(2)}, u32[]{:S(2)}) collective-permute-start(bf16[112,384]{1,0:T(8,128)(2,1)S(1)} %get-tuple-element.38), channel_id=1, source_target_pairs={{0,14},{2,16},{4,18},{6,20},{8,22},{10,24},{12,26},{14,28},{16,30}... | collective-permute-start | bytes 258056 | tf_op jit(solution)/shard_map/apply/ppermute | solution.py:314
  21.2 2.1 %collective-permute-start.7 = (bf16[112,384]{1,0:T(8,128)(2,1)S(1)}, bf16[112,384]{1,0:T(8,128)(2,1)S(1)}, u32[]{:S(2)}, u32[]{:S(2)}) collective-permute-start(bf16[112,384]{1,0:T(8,128)(2,1)S(1)} %get-tuple-element.39), channel_id=1, source_target_pairs={{0,16},{2,18},{4,20},{6,22},{8,24},{10,26},{12,28},{14,30},{16,0},... | collective-permute-start | bytes 258056 | tf_op jit(solution)/shard_map/apply/ppermute | solution.py:314
  23.4 2.4 %load.3 = (bf16[6,384,768]{2,1,0:T(8,128)(2,1)S(1)}, bf16[3,384,384]{2,1,0:T(8,128)(2,1)S(1)}) custom-call(s32[12]{0:T(128)S(1)} %get-tuple-element.31.table, s32[1]{0:T(128)} %bitcast.4.group, bf16[2,6,384,384]{3,2,1,0:T(8,128)(2,1)} %bitcast.33, bf16[2,2,384,384]{3,2,1,0:T(8,128)(2,1)} %bitcast.34), custom_call_target="tpu_custom_call" | custom-call | bytes 4718592 | tf_op jit(solution)/shard_map/load/pallas_call | solution.py:300
  26.1 2.1 %collective-permute-start.9 = (bf16[240,384]{1,0:T(8,128)(2,1)S(1)}, bf16[240,384]{1,0:T(8,128)(2,1)S(1)}, u32[]{:S(2)}, u32[]{:S(2)}) collective-permute-start(bf16[240,384]{1,0:T(8,128)(2,1)S(1)} %get-tuple-element.35.refs_4_), channel_id=1, source_target_pairs={{0,2},{2,0},{4,6},{6,4},{8,10},{10,8},{12,14},{14,12},{16,18},{18,... | collective-permute-start | bytes 552968 | tf_op jit(solution)/shard_map/apply/ppermute | solution.py:314
  28.9 2.8 %collective-permute-done.9.refs_1_.refs_3_ = bf16[240,384]{1,0:T(8,128)(2,1)S(1)} collective-permute-done((bf16[240,384]{1,0:T(8,128)(2,1)S(1)}, bf16[240,384]{1,0:T(8,128)(2,1)S(1)}, u32[]{:S(2)}, u32[]{:S(2)}) %collective-permute-start.9) | collective-permute-done | bytes 184352 | tf_op jit(solution)/shard_map/apply/ppermute | solution.py:314
  32.3 3.9 %collective-permute-start.11 = (bf16[112,384]{1,0:T(8,128)(2,1)S(1)}, bf16[112,384]{1,0:T(8,128)(2,1)S(1)}, u32[]{:S(2)}, u32[]{:S(2)}) collective-permute-start(bf16[112,384]{1,0:T(8,128)(2,1)S(1)} %get-tuple-element.42), channel_id=1, source_target_pairs={{0,28},{2,30},{4,8},{6,10},{8,4},{10,6},{12,16},{14,18},{16,12},{1... | collective-permute-start | bytes 258056 | tf_op jit(solution)/shard_map/apply/ppermute | solution.py:314
  36.2 2.3 %collective-permute-start.12 = (bf16[112,384]{1,0:T(8,128)(2,1)S(1)}, bf16[112,384]{1,0:T(8,128)(2,1)S(1)}, u32[]{:S(2)}, u32[]{:S(2)}) collective-permute-start(bf16[112,384]{1,0:T(8,128)(2,1)S(1)} %get-tuple-element.43), channel_id=1, source_target_pairs={{0,30},{2,4},{4,2},{6,8},{8,6},{10,12},{12,10},{14,16},{16,14},{18... | collective-permute-start | bytes 258056 | tf_op jit(solution)/shard_map/apply/ppermute | solution.py:314
  38.6 1.1 %collective-permute-start.13 = (bf16[112,384]{1,0:T(8,128)(2,1)S(1)}, bf16[112,384]{1,0:T(8,128)(2,1)S(1)}, u32[]{:S(2)}, u32[]{:S(2)}) collective-permute-start(bf16[112,384]{1,0:T(8,128)(2,1)S(1)} %get-tuple-element.44), channel_id=1, source_target_pairs={{0,14},{2,16},{4,18},{6,20},{8,22},{10,24},{12,26},{14,28},{16,30}... | collective-permute-start | bytes 258056 | tf_op jit(solution)/shard_map/apply/ppermute | solution.py:314
  39.7 2.8 %collective-permute-start.14 = (bf16[112,384]{1,0:T(8,128)(2,1)S(1)}, bf16[112,384]{1,0:T(8,128)(2,1)S(1)}, u32[]{:S(2)}, u32[]{:S(2)}) collective-permute-start(bf16[112,384]{1,0:T(8,128)(2,1)S(1)} %get-tuple-element.45), channel_id=1, source_target_pairs={{0,16},{2,18},{4,20},{6,22},{8,24},{10,26},{12,28},{14,30},{16,0},... | collective-permute-start | bytes 258056 | tf_op jit(solution)/shard_map/apply/ppermute | solution.py:314
  43.0 1.5 %collective-permute-done.12.refs_1_ = bf16[112,384]{1,0:T(8,128)(2,1)S(1)} collective-permute-done((bf16[112,384]{1,0:T(8,128)(2,1)S(1)}, bf16[112,384]{1,0:T(8,128)(2,1)S(1)}, u32[]{:S(2)}, u32[]{:S(2)}) %collective-permute-start.12) | collective-permute-done | bytes 86048 | tf_op jit(solution)/shard_map/apply/ppermute | solution.py:314
  47.4 2.2 %collective-permute-start.18 = (bf16[112,384]{1,0:T(8,128)(2,1)S(1)}, bf16[112,384]{1,0:T(8,128)(2,1)S(1)}, u32[]{:S(2)}, u32[]{:S(2)}) collective-permute-start(bf16[112,384]{1,0:T(8,128)(2,1)S(1)} %get-tuple-element.51), channel_id=1, source_target_pairs={{0,28},{2,30},{4,8},{6,10},{8,4},{10,6},{12,16},{14,18},{16,12},{1... | collective-permute-start | bytes 258056 | tf_op jit(solution)/shard_map/apply/ppermute | solution.py:314
  49.6 2.8 %collective-permute-start.19 = (bf16[112,384]{1,0:T(8,128)(2,1)S(1)}, bf16[112,384]{1,0:T(8,128)(2,1)S(1)}, u32[]{:S(2)}, u32[]{:S(2)}) collective-permute-start(bf16[112,384]{1,0:T(8,128)(2,1)S(1)} %get-tuple-element.52), channel_id=1, source_target_pairs={{0,30},{2,4},{4,2},{6,8},{8,6},{10,12},{12,10},{14,16},{16,14},{18... | collective-permute-start | bytes 258056 | tf_op jit(solution)/shard_map/apply/ppermute | solution.py:314
  52.4 3.4 %collective-permute-start.21 = (bf16[112,384]{1,0:T(8,128)(2,1)S(1)}, bf16[112,384]{1,0:T(8,128)(2,1)S(1)}, u32[]{:S(2)}, u32[]{:S(2)}) collective-permute-start(bf16[112,384]{1,0:T(8,128)(2,1)S(1)} %get-tuple-element.54), channel_id=1, source_target_pairs={{0,16},{2,18},{4,20},{6,22},{8,24},{10,26},{12,28},{14,30},{16,0},... | collective-permute-start | bytes 258056 | tf_op jit(solution)/shard_map/apply/ppermute | solution.py:314
  55.8 1.0 %collective-permute-start.23 = (bf16[112,384]{1,0:T(8,128)(2,1)S(1)}, bf16[112,384]{1,0:T(8,128)(2,1)S(1)}, u32[]{:S(2)}, u32[]{:S(2)}) collective-permute-start(bf16[112,384]{1,0:T(8,128)(2,1)S(1)} %get-tuple-element.56), channel_id=1, source_target_pairs={{0,2},{2,0},{4,6},{6,4},{8,10},{10,8},{12,14},{14,12},{16,18},{18,... | collective-permute-start | bytes 258056 | tf_op jit(solution)/shard_map/apply/ppermute | solution.py:314
  56.8 1.7 %collective-permute-done.19.refs_1_ = bf16[112,384]{1,0:T(8,128)(2,1)S(1)} collective-permute-done((bf16[112,384]{1,0:T(8,128)(2,1)S(1)}, bf16[112,384]{1,0:T(8,128)(2,1)S(1)}, u32[]{:S(2)}, u32[]{:S(2)}) %collective-permute-start.19) | collective-permute-done | bytes 86048 | tf_op jit(solution)/shard_map/apply/ppermute | solution.py:314
  61.0 1.1 %apply.25 = (bf16[2,112,384]{2,1,0:T(8,128)(2,1)}, bf16[32,8,112]{2,1,0:T(8,128)(2,1)S(1)}) custom-call(f32[2,112,384]{2,1,0:T(8,128)S(1)} %apply.22.part, f32[2,112,384]{2,1,0:T(8,128)S(1)} %apply.24.far, f32[8,128]{1,0:T(8,128)S(1)} %get-tuple-element.33.asks, bf16[6,384,768]{2,1,0:T(8,128)(2,1)S(1)} %get-tuple-element.34.bands.refs_0_, ...), custom_call_target="tpu_custom_call" | custom-call | flops 33030144 | bytes 165150 | tf_op jit(solution)/shard_map/apply/pallas_call | solution.py:300
  62.1 10.7 %all_to_all.5.pieces = bf16[32,8,112]{2,1,0:T(8,128)(2,1)S(1)} all-to-all(bf16[32,8,112]{2,1,0:T(8,128)(2,1)S(1)} %get-tuple-element.59), channel_id=1, replica_groups=mesh['areal'=16,'layer'=2] {'areal','layer'}, dimensions={0} | all-to-all | bytes 114688 | tf_op jit(solution)/shard_map/project/all_to_all | solution.py:488
  (56 shorter events, 9.5 us)
Async XLA Ops:
  0.6 12.0 %collective-permute-start.3 = (s32[1,1,6]{2,1,0:T(1,128)}, s32[1,1,6]{2,1,0:T(1,128)S(1)}, u32[]{:S(2)}, u32[]{:S(2)}) collective-permute-start(s32[1,1,6]{2,1,0:T(1,128)} %param.13), channel_id=1, source_target_pairs={{16,0},{18,2},{20,4},{22,6},{24,8},{26,10},{28,12},{30,14},{0,16},... | collective-permute-start | bytes 80 | tf_op jit(solution)/shard_map/plan/ppermute | solution.py:370
  4.7 7.9 %collective-permute-start = (s32[1,1,6]{2,1,0:T(1,128)}, s32[1,1,6]{2,1,0:T(1,128)S(1)}, u32[]{:S(2)}, u32[]{:S(2)}) collective-permute-start(s32[1,1,6]{2,1,0:T(1,128)} %param.13), channel_id=1, source_target_pairs={{28,0},{30,2},{8,4},{10,6},{4,8},{6,10},{16,12},{18,14},{12,16},{1... | collective-permute-start | bytes 80 | tf_op jit(solution)/shard_map/plan/ppermute | solution.py:370
  7.0 7.3 %collective-permute-start.1 = (s32[1,1,6]{2,1,0:T(1,128)}, s32[1,1,6]{2,1,0:T(1,128)S(1)}, u32[]{:S(2)}, u32[]{:S(2)}) collective-permute-start(s32[1,1,6]{2,1,0:T(1,128)} %param.13), channel_id=1, source_target_pairs={{30,0},{4,2},{2,4},{8,6},{6,8},{12,10},{10,12},{16,14},{14,16},{20... | collective-permute-start | bytes 80 | tf_op jit(solution)/shard_map/plan/ppermute | solution.py:370
  10.4 5.5 %collective-permute-start.2 = (s32[1,1,6]{2,1,0:T(1,128)}, s32[1,1,6]{2,1,0:T(1,128)S(1)}, u32[]{:S(2)}, u32[]{:S(2)}) collective-permute-start(s32[1,1,6]{2,1,0:T(1,128)} %param.13), channel_id=1, source_target_pairs={{14,0},{16,2},{18,4},{20,6},{22,8},{24,10},{26,12},{28,14},{30,16}... | collective-permute-start | bytes 80 | tf_op jit(solution)/shard_map/plan/ppermute | solution.py:370
  16.6 9.4 %collective-permute-start.4 = (bf16[112,384]{1,0:T(8,128)(2,1)S(1)}, bf16[112,384]{1,0:T(8,128)(2,1)S(1)}, u32[]{:S(2)}, u32[]{:S(2)}) collective-permute-start(bf16[112,384]{1,0:T(8,128)(2,1)S(1)} %get-tuple-element.36), channel_id=1, source_target_pairs={{0,28},{2,30},{4,8},{6,10},{8,4},{10,6},{12,16},{14,18},{16,12},{1... | collective-permute-start | bytes 258056 | tf_op jit(solution)/shard_map/apply/ppermute | solution.py:314
  17.1 11.1 %collective-permute-start.5 = (bf16[112,384]{1,0:T(8,128)(2,1)S(1)}, bf16[112,384]{1,0:T(8,128)(2,1)S(1)}, u32[]{:S(2)}, u32[]{:S(2)}) collective-permute-start(bf16[112,384]{1,0:T(8,128)(2,1)S(1)} %get-tuple-element.37), channel_id=1, source_target_pairs={{0,30},{2,4},{4,2},{6,8},{8,6},{10,12},{12,10},{14,16},{16,14},{18... | collective-permute-start | bytes 258056 | tf_op jit(solution)/shard_map/apply/ppermute | solution.py:314
  19.9 8.6 %collective-permute-start.6 = (bf16[112,384]{1,0:T(8,128)(2,1)S(1)}, bf16[112,384]{1,0:T(8,128)(2,1)S(1)}, u32[]{:S(2)}, u32[]{:S(2)}) collective-permute-start(bf16[112,384]{1,0:T(8,128)(2,1)S(1)} %get-tuple-element.38), channel_id=1, source_target_pairs={{0,14},{2,16},{4,18},{6,20},{8,22},{10,24},{12,26},{14,28},{16,30}... | collective-permute-start | bytes 258056 | tf_op jit(solution)/shard_map/apply/ppermute | solution.py:314
  21.2 7.4 %collective-permute-start.7 = (bf16[112,384]{1,0:T(8,128)(2,1)S(1)}, bf16[112,384]{1,0:T(8,128)(2,1)S(1)}, u32[]{:S(2)}, u32[]{:S(2)}) collective-permute-start(bf16[112,384]{1,0:T(8,128)(2,1)S(1)} %get-tuple-element.39), channel_id=1, source_target_pairs={{0,16},{2,18},{4,20},{6,22},{8,24},{10,26},{12,28},{14,30},{16,0},... | collective-permute-start | bytes 258056 | tf_op jit(solution)/shard_map/apply/ppermute | solution.py:314
  23.3 5.6 %collective-permute-start.8 = (bf16[240,384]{1,0:T(8,128)(2,1)S(1)}, bf16[240,384]{1,0:T(8,128)(2,1)S(1)}, u32[]{:S(2)}, u32[]{:S(2)}) collective-permute-start(bf16[240,384]{1,0:T(8,128)(2,1)S(1)} %get-tuple-element.35.refs_4_), channel_id=1, source_target_pairs={{0,4},{2,6},{4,0},{6,2},{8,12},{10,14},{12,8},{14,10},{16,20},{18,... | collective-permute-start | bytes 552968 | tf_op jit(solution)/shard_map/apply/ppermute | solution.py:314
  26.1 5.6 %collective-permute-start.9 = (bf16[240,384]{1,0:T(8,128)(2,1)S(1)}, bf16[240,384]{1,0:T(8,128)(2,1)S(1)}, u32[]{:S(2)}, u32[]{:S(2)}) collective-permute-start(bf16[240,384]{1,0:T(8,128)(2,1)S(1)} %get-tuple-element.35.refs_4_), channel_id=1, source_target_pairs={{0,2},{2,0},{4,6},{6,4},{8,10},{10,8},{12,14},{14,12},{16,18},{18,... | collective-permute-start | bytes 552968 | tf_op jit(solution)/shard_map/apply/ppermute | solution.py:314
  28.2 3.5 %collective-permute-start.10 = (bf16[240,384]{1,0:T(8,128)(2,1)S(1)}, bf16[240,384]{1,0:T(8,128)(2,1)S(1)}, u32[]{:S(2)}, u32[]{:S(2)}) collective-permute-start(bf16[240,384]{1,0:T(8,128)(2,1)S(1)} %get-tuple-element.35.refs_4_), channel_id=1, source_target_pairs={{0,1},{1,0},{2,3},{3,2},{4,5},{5,4},{6,7},{7,6},{8,9},{9,8},{10,11... | collective-permute-start | bytes 552968 | tf_op jit(solution)/shard_map/apply/ppermute | solution.py:324
  32.3 10.1 %collective-permute-start.11 = (bf16[112,384]{1,0:T(8,128)(2,1)S(1)}, bf16[112,384]{1,0:T(8,128)(2,1)S(1)}, u32[]{:S(2)}, u32[]{:S(2)}) collective-permute-start(bf16[112,384]{1,0:T(8,128)(2,1)S(1)} %get-tuple-element.42), channel_id=1, source_target_pairs={{0,28},{2,30},{4,8},{6,10},{8,4},{10,6},{12,16},{14,18},{16,12},{1... | collective-permute-start | bytes 258056 | tf_op jit(solution)/shard_map/apply/ppermute | solution.py:314
  36.2 8.2 %collective-permute-start.12 = (bf16[112,384]{1,0:T(8,128)(2,1)S(1)}, bf16[112,384]{1,0:T(8,128)(2,1)S(1)}, u32[]{:S(2)}, u32[]{:S(2)}) collective-permute-start(bf16[112,384]{1,0:T(8,128)(2,1)S(1)} %get-tuple-element.43), channel_id=1, source_target_pairs={{0,30},{2,4},{4,2},{6,8},{8,6},{10,12},{12,10},{14,16},{16,14},{18... | collective-permute-start | bytes 258056 | tf_op jit(solution)/shard_map/apply/ppermute | solution.py:314
  38.6 7.2 %collective-permute-start.13 = (bf16[112,384]{1,0:T(8,128)(2,1)S(1)}, bf16[112,384]{1,0:T(8,128)(2,1)S(1)}, u32[]{:S(2)}, u32[]{:S(2)}) collective-permute-start(bf16[112,384]{1,0:T(8,128)(2,1)S(1)} %get-tuple-element.44), channel_id=1, source_target_pairs={{0,14},{2,16},{4,18},{6,20},{8,22},{10,24},{12,26},{14,28},{16,30}... | collective-permute-start | bytes 258056 | tf_op jit(solution)/shard_map/apply/ppermute | solution.py:314
  39.7 6.3 %collective-permute-start.14 = (bf16[112,384]{1,0:T(8,128)(2,1)S(1)}, bf16[112,384]{1,0:T(8,128)(2,1)S(1)}, u32[]{:S(2)}, u32[]{:S(2)}) collective-permute-start(bf16[112,384]{1,0:T(8,128)(2,1)S(1)} %get-tuple-element.45), channel_id=1, source_target_pairs={{0,16},{2,18},{4,20},{6,22},{8,24},{10,26},{12,28},{14,30},{16,0},... | collective-permute-start | bytes 258056 | tf_op jit(solution)/shard_map/apply/ppermute | solution.py:314
  42.4 4.5 %collective-permute-start.15 = (bf16[112,384]{1,0:T(8,128)(2,1)S(1)}, bf16[112,384]{1,0:T(8,128)(2,1)S(1)}, u32[]{:S(2)}, u32[]{:S(2)}) collective-permute-start(bf16[112,384]{1,0:T(8,128)(2,1)S(1)} %get-tuple-element.46), channel_id=1, source_target_pairs={{0,4},{2,6},{4,0},{6,2},{8,12},{10,14},{12,8},{14,10},{16,20},{18,... | collective-permute-start | bytes 258056 | tf_op jit(solution)/shard_map/apply/ppermute | solution.py:314
  42.4 4.5 %collective-permute-start.16 = (bf16[112,384]{1,0:T(8,128)(2,1)S(1)}, bf16[112,384]{1,0:T(8,128)(2,1)S(1)}, u32[]{:S(2)}, u32[]{:S(2)}) collective-permute-start(bf16[112,384]{1,0:T(8,128)(2,1)S(1)} %get-tuple-element.47), channel_id=1, source_target_pairs={{0,2},{2,0},{4,6},{6,4},{8,10},{10,8},{12,14},{14,12},{16,18},{18,... | collective-permute-start | bytes 258056 | tf_op jit(solution)/shard_map/apply/ppermute | solution.py:314
  47.4 8.4 %collective-permute-start.18 = (bf16[112,384]{1,0:T(8,128)(2,1)S(1)}, bf16[112,384]{1,0:T(8,128)(2,1)S(1)}, u32[]{:S(2)}, u32[]{:S(2)}) collective-permute-start(bf16[112,384]{1,0:T(8,128)(2,1)S(1)} %get-tuple-element.51), channel_id=1, source_target_pairs={{0,28},{2,30},{4,8},{6,10},{8,4},{10,6},{12,16},{14,18},{16,12},{1... | collective-permute-start | bytes 258056 | tf_op jit(solution)/shard_map/apply/ppermute | solution.py:314
  49.6 8.9 %collective-permute-start.19 = (bf16[112,384]{1,0:T(8,128)(2,1)S(1)}, bf16[112,384]{1,0:T(8,128)(2,1)S(1)}, u32[]{:S(2)}, u32[]{:S(2)}) collective-permute-start(bf16[112,384]{1,0:T(8,128)(2,1)S(1)} %get-tuple-element.52), channel_id=1, source_target_pairs={{0,30},{2,4},{4,2},{6,8},{8,6},{10,12},{12,10},{14,16},{16,14},{18... | collective-permute-start | bytes 258056 | tf_op jit(solution)/shard_map/apply/ppermute | solution.py:314
  52.4 7.8 %collective-permute-start.20 = (bf16[112,384]{1,0:T(8,128)(2,1)S(1)}, bf16[112,384]{1,0:T(8,128)(2,1)S(1)}, u32[]{:S(2)}, u32[]{:S(2)}) collective-permute-start(bf16[112,384]{1,0:T(8,128)(2,1)S(1)} %get-tuple-element.53), channel_id=1, source_target_pairs={{0,14},{2,16},{4,18},{6,20},{8,22},{10,24},{12,26},{14,28},{16,30}... | collective-permute-start | bytes 258056 | tf_op jit(solution)/shard_map/apply/ppermute | solution.py:314
  52.4 7.8 %collective-permute-start.21 = (bf16[112,384]{1,0:T(8,128)(2,1)S(1)}, bf16[112,384]{1,0:T(8,128)(2,1)S(1)}, u32[]{:S(2)}, u32[]{:S(2)}) collective-permute-start(bf16[112,384]{1,0:T(8,128)(2,1)S(1)} %get-tuple-element.54), channel_id=1, source_target_pairs={{0,16},{2,18},{4,20},{6,22},{8,24},{10,26},{12,28},{14,30},{16,0},... | collective-permute-start | bytes 258056 | tf_op jit(solution)/shard_map/apply/ppermute | solution.py:314
  55.8 4.7 %collective-permute-start.22 = (bf16[112,384]{1,0:T(8,128)(2,1)S(1)}, bf16[112,384]{1,0:T(8,128)(2,1)S(1)}, u32[]{:S(2)}, u32[]{:S(2)}) collective-permute-start(bf16[112,384]{1,0:T(8,128)(2,1)S(1)} %get-tuple-element.55), channel_id=1, source_target_pairs={{0,4},{2,6},{4,0},{6,2},{8,12},{10,14},{12,8},{14,10},{16,20},{18,... | collective-permute-start | bytes 258056 | tf_op jit(solution)/shard_map/apply/ppermute | solution.py:314
  55.8 5.2 %collective-permute-start.23 = (bf16[112,384]{1,0:T(8,128)(2,1)S(1)}, bf16[112,384]{1,0:T(8,128)(2,1)S(1)}, u32[]{:S(2)}, u32[]{:S(2)}) collective-permute-start(bf16[112,384]{1,0:T(8,128)(2,1)S(1)} %get-tuple-element.56), channel_id=1, source_target_pairs={{0,2},{2,0},{4,6},{6,4},{8,10},{10,8},{12,14},{14,12},{16,18},{18,... | collective-permute-start | bytes 258056 | tf_op jit(solution)/shard_map/apply/ppermute | solution.py:314
  58.5 2.5 %collective-permute-start.24 = (bf16[112,384]{1,0:T(8,128)(2,1)S(1)}, bf16[112,384]{1,0:T(8,128)(2,1)S(1)}, u32[]{:S(2)}, u32[]{:S(2)}) collective-permute-start(bf16[112,384]{1,0:T(8,128)(2,1)S(1)} %get-tuple-element.57), channel_id=1, source_target_pairs={{0,1},{1,0},{2,3},{3,2},{4,5},{5,4},{6,7},{7,6},{8,9},{9,8},{10,11... | collective-permute-start | bytes 258056 | tf_op jit(solution)/shard_map/apply/ppermute | solution.py:324
  (6 other events, 76.8 us)
where the time goes:
time: 74 us; the launch traced here: 73.5 us
  starting transfers between devices  38.6 us (52%)
  waiting for transfers between devices  11.4 us (15%)
  Pallas kernels  11.2 us (15%)
  blocking collectives  10.7 us (14%)
  between operations  1.55 us (2%)
    ppermute x18, starting transfers between devices, moved_by(): return held(lax.ppermute(x, 'areal', pairs))  28.9 us
    pallas_call x19, Pallas kernels, call(): pl.pallas_call(kernel, out_shape=outs, in_specs=specs, out_specs=out_spec...  11.2 us
    all_to_all x1, blocking collectives, on_device(): landed = lax.all_to_all(pieces, ('areal', 'layer'), 0, 0, tiled=True)  10.7 us
    ppermute x4, starting transfers between devices, on_device(): lax.ppermute(conn_src, 'areal', [(to, at) for at, to in routes[i]])  9.75 us
    ppermute x18, waiting for transfers between devices, moved_by(): return held(lax.ppermute(x, 'areal', pairs))  8.22 us
    ppermute x4, waiting for transfers between devices, on_device(): lax.ppermute(conn_src, 'areal', [(to, at) for at, to in routes[i]])  3.2 us
  transfers between devices with their start and end apart: 25, of which 10 were waited for; matrix products, arithmetic and copies ran while one was open for 0% of the time, Pallas kernels for 10%

commit v1 on v0

--- a/solution.py
+++ b/solution.py
@@ -149,7 +149,7 @@
 
 def cross_pick_kernel(lines, me, tile_map, *refs):
     count = len(lines)
-    tables, payload, known, tiles = refs[:count], refs[count], refs[count + 1], refs[count + 2 :]
+    tables, (payload, _, known), tiles = refs[:count], refs[count : count + 3], refs[count + 3 :]
     rows = tiles[0].shape[0]
     line = lax.broadcasted_iota(jnp.int32, known.shape, 0)
     masks = jnp.zeros(known.shape, F32)
@@ -381,13 +381,6 @@
             out_specs=[SMEM] + [VMEM] * 2,
         )
         asks, payload = held(asks), held(payload)
-        known, *crossing = call(
-            partial(cross_pick_kernel, lines),
-            [masks_type] + [tile] * len(lines),
-            (me, outside(tile_map), *[x[0, 0] for x in tables], payload),
-            [SMEM] * (2 + len(lines)) + [VMEM],
-        )
-        known = held(known)
 
     with jax.named_scope("load"):
         bands, sides = call(
@@ -402,6 +395,13 @@
             moved=areal_blocks.size * 2 + vertical_blocks.size * 2,
         )
         bands, sides = held(bands), held(sides)
+        known, *crossing = call(
+            partial(cross_pick_kernel, lines),
+            [masks_type] + [tile] * len(lines),
+            (me, outside(tile_map), *[x[0, 0] for x in tables], payload, sides),
+            [SMEM] * (2 + len(lines)) + [VMEM] * 2,
+        )
+        known = held(known)
         (factors,) = call(
             weigh_kernel,
             [pltpu.VMEM((sens.shape[2], 2, sens.shape[3]), F32)],

time: 74 us -> 74.5 us (level)
  waiting for transfers between devices: 11.4 us -> 10.3 us
  blocking collectives: 10.7 us -> 11.5 us
    ppermute x4, waiting for transfers between devices: 3.2 us -> 0.63 us  [on_device(): lax.ppermute(conn_src, 'areal', [(to, at) for at, to in routes[i]])]
    ppermute x18, waiting for transfers between devices: 8.22 us -> 9.65 us  [moved_by(): return held(lax.ppermute(x, 'areal', pairs))]
  transfers between devices with their start and end apart: 25 -> 25, of which waited for: 10 -> 9; matrix products, arithmetic and copies ran while one was open for 0% -> 0% of each run, Pallas kernels for 10% -> 10%
where the time goes in v1:
time: 74.5 us; the launch traced here: 74 us
  starting transfers between devices  39.3 us (53%)
  blocking collectives  11.5 us (15%)
  Pallas kernels  11.3 us (15%)
  waiting for transfers between devices  10.3 us (14%)
  between operations  1.55 us (2%)
    ppermute x18, starting transfers between devices, moved_by(): return held(lax.ppermute(x, 'areal', pairs))  29.5 us
    all_to_all x1, blocking collectives, on_device(): landed = lax.all_to_all(pieces, ('areal', 'layer'), 0, 0, tiled=True)  11.5 us
    pallas_call x19, Pallas kernels, call(): pl.pallas_call(kernel, out_shape=outs, in_specs=specs, out_specs=out_spec...  11.3 us
    ppermute x4, starting transfers between devices, on_device(): lax.ppermute(conn_src, 'areal', [(to, at) for at, to in routes[i]])  9.75 us
    ppermute x18, waiting for transfers between devices, moved_by(): return held(lax.ppermute(x, 'areal', pairs))  9.65 us
  transfers between devices with their start and end apart: 25, of which 9 were waited for; matrix products, arithmetic and copies ran while one was open for 0% of the time, Pallas kernels for 10%

profile of v1, /device:TPU:0, one launch (start us, length us, event | category | flops | bytes accessed | tf_op | source)
XLA Modules:
  0.0 74.0 jit_solution(12909908839564411482)
XLA Ops:
  0.6 4.1 %collective-permute-start.3 = (s32[1,1,6]{2,1,0:T(1,128)}, s32[1,1,6]{2,1,0:T(1,128)S(1)}, u32[]{:S(2)}, u32[]{:S(2)}) collective-permute-start(s32[1,1,6]{2,1,0:T(1,128)} %param.13), channel_id=1, source_target_pairs={{16,0},{18,2},{20,4},{22,6},{24,8},{26,10},{28,12},{30,14},{0,16},... | collective-permute-start | bytes 80 | tf_op jit(solution)/shard_map/plan/ppermute | solution.py:370
  4.7 2.3 %collective-permute-start = (s32[1,1,6]{2,1,0:T(1,128)}, s32[1,1,6]{2,1,0:T(1,128)S(1)}, u32[]{:S(2)}, u32[]{:S(2)}) collective-permute-start(s32[1,1,6]{2,1,0:T(1,128)} %param.13), channel_id=1, source_target_pairs={{28,0},{30,2},{8,4},{10,6},{4,8},{6,10},{16,12},{18,14},{12,16},{1... | collective-permute-start | bytes 80 | tf_op jit(solution)/shard_map/plan/ppermute | solution.py:370
  7.0 3.3 %collective-permute-start.1 = (s32[1,1,6]{2,1,0:T(1,128)}, s32[1,1,6]{2,1,0:T(1,128)S(1)}, u32[]{:S(2)}, u32[]{:S(2)}) collective-permute-start(s32[1,1,6]{2,1,0:T(1,128)} %param.13), channel_id=1, source_target_pairs={{30,0},{4,2},{2,4},{8,6},{6,8},{12,10},{10,12},{16,14},{14,16},{20... | collective-permute-start | bytes 80 | tf_op jit(solution)/shard_map/plan/ppermute | solution.py:370
  11.0 1.6 %plan.1 = (s32[12]{0:T(128)S(1)}, f32[8,128]{1,0:T(8,128)S(1)}, bf16[240,384]{1,0:T(8,128)(2,1)S(1)}) custom-call(s32[6]{0:T(128)} %bitcast.36, s32[1]{0:T(128)} %bitcast.19.count, s32[32]{0:T(128)} %tile_map.3, s32[1]{0:T(128)} %bitcast.3.me, s32[1]{0:T(128)} %bitcast.4.group, bf16[224,384]{1,0:T(8,128)(2,1)} %bitcast.20), custom_call_target="tpu_custom_call" | custom-call | tf_op jit(solution)/shard_map/plan/pallas_call | solution.py:300
  12.7 2.6 %load.4 = (bf16[6,384,768]{2,1,0:T(8,128)(2,1)S(1)}, bf16[3,384,384]{2,1,0:T(8,128)(2,1)S(1)}) custom-call(s32[12]{0:T(128)S(1)} %get-tuple-element.31.table, s32[1]{0:T(128)} %bitcast.4.group, bf16[2,6,384,384]{3,2,1,0:T(8,128)(2,1)} %bitcast.33, bf16[2,2,384,384]{3,2,1,0:T(8,128)(2,1)} %bitcast.34), custom_call_target="tpu_custom_call" | custom-call | bytes 4718592 | tf_op jit(solution)/shard_map/load/pallas_call | solution.py:300
  16.6 2.7 %collective-permute-start.4 = (bf16[112,384]{1,0:T(8,128)(2,1)S(1)}, bf16[112,384]{1,0:T(8,128)(2,1)S(1)}, u32[]{:S(2)}, u32[]{:S(2)}) collective-permute-start(bf16[112,384]{1,0:T(8,128)(2,1)S(1)} %get-tuple-element.36), channel_id=1, source_target_pairs={{0,28},{2,30},{4,8},{6,10},{8,4},{10,6},{12,16},{14,18},{16,12},{1... | collective-permute-start | bytes 258056 | tf_op jit(solution)/shard_map/apply/ppermute | solution.py:314
  19.4 2.8 %collective-permute-start.5 = (bf16[112,384]{1,0:T(8,128)(2,1)S(1)}, bf16[112,384]{1,0:T(8,128)(2,1)S(1)}, u32[]{:S(2)}, u32[]{:S(2)}) collective-permute-start(bf16[112,384]{1,0:T(8,128)(2,1)S(1)} %get-tuple-element.37), channel_id=1, source_target_pairs={{0,30},{2,4},{4,2},{6,8},{8,6},{10,12},{12,10},{14,16},{16,14},{18... | collective-permute-start | bytes 258056 | tf_op jit(solution)/shard_map/apply/ppermute | solution.py:314
  22.1 1.0 %collective-permute-start.6 = (bf16[112,384]{1,0:T(8,128)(2,1)S(1)}, bf16[112,384]{1,0:T(8,128)(2,1)S(1)}, u32[]{:S(2)}, u32[]{:S(2)}) collective-permute-start(bf16[112,384]{1,0:T(8,128)(2,1)S(1)} %get-tuple-element.38), channel_id=1, source_target_pairs={{0,14},{2,16},{4,18},{6,20},{8,22},{10,24},{12,26},{14,28},{16,30}... | collective-permute-start | bytes 258056 | tf_op jit(solution)/shard_map/apply/ppermute | solution.py:314
  23.1 2.4 %collective-permute-start.7 = (bf16[112,384]{1,0:T(8,128)(2,1)S(1)}, bf16[112,384]{1,0:T(8,128)(2,1)S(1)}, u32[]{:S(2)}, u32[]{:S(2)}) collective-permute-start(bf16[112,384]{1,0:T(8,128)(2,1)S(1)} %get-tuple-element.39), channel_id=1, source_target_pairs={{0,16},{2,18},{4,20},{6,22},{8,24},{10,26},{12,28},{14,30},{16,0},... | collective-permute-start | bytes 258056 | tf_op jit(solution)/shard_map/apply/ppermute | solution.py:314
  25.8 1.0 %collective-permute-start.9 = (bf16[240,384]{1,0:T(8,128)(2,1)S(1)}, bf16[240,384]{1,0:T(8,128)(2,1)S(1)}, u32[]{:S(2)}, u32[]{:S(2)}) collective-permute-start(bf16[240,384]{1,0:T(8,128)(2,1)S(1)} %get-tuple-element.35.refs_4_), channel_id=1, source_target_pairs={{0,2},{2,0},{4,6},{6,4},{8,10},{10,8},{12,14},{14,12},{16,18},{18,... | collective-permute-start | bytes 552968 | tf_op jit(solution)/shard_map/apply/ppermute | solution.py:314
  26.9 1.6 %collective-permute-done.5.refs_1_ = bf16[112,384]{1,0:T(8,128)(2,1)S(1)} collective-permute-done((bf16[112,384]{1,0:T(8,128)(2,1)S(1)}, bf16[112,384]{1,0:T(8,128)(2,1)S(1)}, u32[]{:S(2)}, u32[]{:S(2)}) %collective-permute-start.5) | collective-permute-done | bytes 86048 | tf_op jit(solution)/shard_map/apply/ppermute | solution.py:314
  28.8 1.5 %collective-permute-done.6.refs_0_ = bf16[112,384]{1,0:T(8,128)(2,1)S(1)} collective-permute-done((bf16[112,384]{1,0:T(8,128)(2,1)S(1)}, bf16[112,384]{1,0:T(8,128)(2,1)S(1)}, u32[]{:S(2)}, u32[]{:S(2)}) %collective-permute-start.6) | collective-permute-done | bytes 86048 | tf_op jit(solution)/shard_map/apply/ppermute | solution.py:314
  32.5 2.3 %collective-permute-start.11 = (bf16[112,384]{1,0:T(8,128)(2,1)S(1)}, bf16[112,384]{1,0:T(8,128)(2,1)S(1)}, u32[]{:S(2)}, u32[]{:S(2)}) collective-permute-start(bf16[112,384]{1,0:T(8,128)(2,1)S(1)} %get-tuple-element.42), channel_id=1, source_target_pairs={{0,28},{2,30},{4,8},{6,10},{8,4},{10,6},{12,16},{14,18},{16,12},{1... | collective-permute-start | bytes 258056 | tf_op jit(solution)/shard_map/apply/ppermute | solution.py:314
  34.8 2.5 %collective-permute-start.12 = (bf16[112,384]{1,0:T(8,128)(2,1)S(1)}, bf16[112,384]{1,0:T(8,128)(2,1)S(1)}, u32[]{:S(2)}, u32[]{:S(2)}) collective-permute-start(bf16[112,384]{1,0:T(8,128)(2,1)S(1)} %get-tuple-element.43), channel_id=1, source_target_pairs={{0,30},{2,4},{4,2},{6,8},{8,6},{10,12},{12,10},{14,16},{16,14},{18... | collective-permute-start | bytes 258056 | tf_op jit(solution)/shard_map/apply/ppermute | solution.py:314
  37.3 3.7 %collective-permute-start.14 = (bf16[112,384]{1,0:T(8,128)(2,1)S(1)}, bf16[112,384]{1,0:T(8,128)(2,1)S(1)}, u32[]{:S(2)}, u32[]{:S(2)}) collective-permute-start(bf16[112,384]{1,0:T(8,128)(2,1)S(1)} %get-tuple-element.45), channel_id=1, source_target_pairs={{0,16},{2,18},{4,20},{6,22},{8,24},{10,26},{12,28},{14,30},{16,0},... | collective-permute-start | bytes 258056 | tf_op jit(solution)/shard_map/apply/ppermute | solution.py:314
  41.7 1.7 %collective-permute-done.12.refs_1_ = bf16[112,384]{1,0:T(8,128)(2,1)S(1)} collective-permute-done((bf16[112,384]{1,0:T(8,128)(2,1)S(1)}, bf16[112,384]{1,0:T(8,128)(2,1)S(1)}, u32[]{:S(2)}, u32[]{:S(2)}) %collective-permute-start.12) | collective-permute-done | bytes 86048 | tf_op jit(solution)/shard_map/apply/ppermute | solution.py:314
  44.0 1.5 %collective-permute-done.13.refs_0_ = bf16[112,384]{1,0:T(8,128)(2,1)S(1)} collective-permute-done((bf16[112,384]{1,0:T(8,128)(2,1)S(1)}, bf16[112,384]{1,0:T(8,128)(2,1)S(1)}, u32[]{:S(2)}, u32[]{:S(2)}) %collective-permute-start.13) | collective-permute-done | bytes 86048 | tf_op jit(solution)/shard_map/apply/ppermute | solution.py:314
  46.4 2.9 %collective-permute-start.18 = (bf16[112,384]{1,0:T(8,128)(2,1)S(1)}, bf16[112,384]{1,0:T(8,128)(2,1)S(1)}, u32[]{:S(2)}, u32[]{:S(2)}) collective-permute-start(bf16[112,384]{1,0:T(8,128)(2,1)S(1)} %get-tuple-element.51), channel_id=1, source_target_pairs={{0,28},{2,30},{4,8},{6,10},{8,4},{10,6},{12,16},{14,18},{16,12},{1... | collective-permute-start | bytes 258056 | tf_op jit(solution)/shard_map/apply/ppermute | solution.py:314
  49.3 3.2 %collective-permute-start.19 = (bf16[112,384]{1,0:T(8,128)(2,1)S(1)}, bf16[112,384]{1,0:T(8,128)(2,1)S(1)}, u32[]{:S(2)}, u32[]{:S(2)}) collective-permute-start(bf16[112,384]{1,0:T(8,128)(2,1)S(1)} %get-tuple-element.52), channel_id=1, source_target_pairs={{0,30},{2,4},{4,2},{6,8},{8,6},{10,12},{12,10},{14,16},{16,14},{18... | collective-permute-start | bytes 258056 | tf_op jit(solution)/shard_map/apply/ppermute | solution.py:314
  52.7 2.8 %collective-permute-start.21 = (bf16[112,384]{1,0:T(8,128)(2,1)S(1)}, bf16[112,384]{1,0:T(8,128)(2,1)S(1)}, u32[]{:S(2)}, u32[]{:S(2)}) collective-permute-start(bf16[112,384]{1,0:T(8,128)(2,1)S(1)} %get-tuple-element.54), channel_id=1, source_target_pairs={{0,16},{2,18},{4,20},{6,22},{8,24},{10,26},{12,28},{14,30},{16,0},... | collective-permute-start | bytes 258056 | tf_op jit(solution)/shard_map/apply/ppermute | solution.py:314
  55.5 1.4 %collective-permute-start.23 = (bf16[112,384]{1,0:T(8,128)(2,1)S(1)}, bf16[112,384]{1,0:T(8,128)(2,1)S(1)}, u32[]{:S(2)}, u32[]{:S(2)}) collective-permute-start(bf16[112,384]{1,0:T(8,128)(2,1)S(1)} %get-tuple-element.56), channel_id=1, source_target_pairs={{0,2},{2,0},{4,6},{6,4},{8,10},{10,8},{12,14},{14,12},{16,18},{18,... | collective-permute-start | bytes 258056 | tf_op jit(solution)/shard_map/apply/ppermute | solution.py:314
  56.9 1.5 %collective-permute-done.19.refs_1_ = bf16[112,384]{1,0:T(8,128)(2,1)S(1)} collective-permute-done((bf16[112,384]{1,0:T(8,128)(2,1)S(1)}, bf16[112,384]{1,0:T(8,128)(2,1)S(1)}, u32[]{:S(2)}, u32[]{:S(2)}) %collective-permute-start.19) | collective-permute-done | bytes 86048 | tf_op jit(solution)/shard_map/apply/ppermute | solution.py:314
  60.7 1.1 %apply.25 = (bf16[2,112,384]{2,1,0:T(8,128)(2,1)}, bf16[32,8,112]{2,1,0:T(8,128)(2,1)S(1)}) custom-call(f32[2,112,384]{2,1,0:T(8,128)S(1)} %apply.22.part, f32[2,112,384]{2,1,0:T(8,128)S(1)} %apply.24.far, f32[8,128]{1,0:T(8,128)S(1)} %get-tuple-element.33.asks, bf16[6,384,768]{2,1,0:T(8,128)(2,1)S(1)} %get-tuple-element.34.bands.refs_0_, ...), custom_call_target="tpu_custom_call" | custom-call | flops 33030144 | bytes 165150 | tf_op jit(solution)/shard_map/apply/pallas_call | solution.py:300
  61.8 11.5 %all_to_all.5.pieces = bf16[32,8,112]{2,1,0:T(8,128)(2,1)S(1)} all-to-all(bf16[32,8,112]{2,1,0:T(8,128)(2,1)S(1)} %get-tuple-element.59), channel_id=1, replica_groups=mesh['areal'=16,'layer'=2] {'areal','layer'}, dimensions={0} | all-to-all | bytes 114688 | tf_op jit(solution)/shard_map/project/all_to_all | solution.py:488
  (56 shorter events, 9.7 us)
Async XLA Ops:
  0.6 14.6 %collective-permute-start.3 = (s32[1,1,6]{2,1,0:T(1,128)}, s32[1,1,6]{2,1,0:T(1,128)S(1)}, u32[]{:S(2)}, u32[]{:S(2)}) collective-permute-start(s32[1,1,6]{2,1,0:T(1,128)} %param.13), channel_id=1, source_target_pairs={{16,0},{18,2},{20,4},{22,6},{24,8},{26,10},{28,12},{30,14},{0,16},... | collective-permute-start | bytes 80 | tf_op jit(solution)/shard_map/plan/ppermute | solution.py:370
  4.7 10.5 %collective-permute-start = (s32[1,1,6]{2,1,0:T(1,128)}, s32[1,1,6]{2,1,0:T(1,128)S(1)}, u32[]{:S(2)}, u32[]{:S(2)}) collective-permute-start(s32[1,1,6]{2,1,0:T(1,128)} %param.13), channel_id=1, source_target_pairs={{28,0},{30,2},{8,4},{10,6},{4,8},{6,10},{16,12},{18,14},{12,16},{1... | collective-permute-start | bytes 80 | tf_op jit(solution)/shard_map/plan/ppermute | solution.py:370
  7.0 8.2 %collective-permute-start.1 = (s32[1,1,6]{2,1,0:T(1,128)}, s32[1,1,6]{2,1,0:T(1,128)S(1)}, u32[]{:S(2)}, u32[]{:S(2)}) collective-permute-start(s32[1,1,6]{2,1,0:T(1,128)} %param.13), channel_id=1, source_target_pairs={{30,0},{4,2},{2,4},{8,6},{6,8},{12,10},{10,12},{16,14},{14,16},{20... | collective-permute-start | bytes 80 | tf_op jit(solution)/shard_map/plan/ppermute | solution.py:370
  10.4 5.5 %collective-permute-start.2 = (s32[1,1,6]{2,1,0:T(1,128)}, s32[1,1,6]{2,1,0:T(1,128)S(1)}, u32[]{:S(2)}, u32[]{:S(2)}) collective-permute-start(s32[1,1,6]{2,1,0:T(1,128)} %param.13), channel_id=1, source_target_pairs={{14,0},{16,2},{18,4},{20,6},{22,8},{24,10},{26,12},{28,14},{30,16}... | collective-permute-start | bytes 80 | tf_op jit(solution)/shard_map/plan/ppermute | solution.py:370
  16.6 9.2 %collective-permute-start.4 = (bf16[112,384]{1,0:T(8,128)(2,1)S(1)}, bf16[112,384]{1,0:T(8,128)(2,1)S(1)}, u32[]{:S(2)}, u32[]{:S(2)}) collective-permute-start(bf16[112,384]{1,0:T(8,128)(2,1)S(1)} %get-tuple-element.36), channel_id=1, source_target_pairs={{0,28},{2,30},{4,8},{6,10},{8,4},{10,6},{12,16},{14,18},{16,12},{1... | collective-permute-start | bytes 258056 | tf_op jit(solution)/shard_map/apply/ppermute | solution.py:314
  19.4 9.1 %collective-permute-start.5 = (bf16[112,384]{1,0:T(8,128)(2,1)S(1)}, bf16[112,384]{1,0:T(8,128)(2,1)S(1)}, u32[]{:S(2)}, u32[]{:S(2)}) collective-permute-start(bf16[112,384]{1,0:T(8,128)(2,1)S(1)} %get-tuple-element.37), channel_id=1, source_target_pairs={{0,30},{2,4},{4,2},{6,8},{8,6},{10,12},{12,10},{14,16},{16,14},{18... | collective-permute-start | bytes 258056 | tf_op jit(solution)/shard_map/apply/ppermute | solution.py:314
  22.1 8.1 %collective-permute-start.6 = (bf16[112,384]{1,0:T(8,128)(2,1)S(1)}, bf16[112,384]{1,0:T(8,128)(2,1)S(1)}, u32[]{:S(2)}, u32[]{:S(2)}) collective-permute-start(bf16[112,384]{1,0:T(8,128)(2,1)S(1)} %get-tuple-element.38), channel_id=1, source_target_pairs={{0,14},{2,16},{4,18},{6,20},{8,22},{10,24},{12,26},{14,28},{16,30}... | collective-permute-start | bytes 258056 | tf_op jit(solution)/shard_map/apply/ppermute | solution.py:314
  23.1 7.1 %collective-permute-start.7 = (bf16[112,384]{1,0:T(8,128)(2,1)S(1)}, bf16[112,384]{1,0:T(8,128)(2,1)S(1)}, u32[]{:S(2)}, u32[]{:S(2)}) collective-permute-start(bf16[112,384]{1,0:T(8,128)(2,1)S(1)} %get-tuple-element.39), channel_id=1, source_target_pairs={{0,16},{2,18},{4,20},{6,22},{8,24},{10,26},{12,28},{14,30},{16,0},... | collective-permute-start | bytes 258056 | tf_op jit(solution)/shard_map/apply/ppermute | solution.py:314
  25.5 5.5 %collective-permute-start.8 = (bf16[240,384]{1,0:T(8,128)(2,1)S(1)}, bf16[240,384]{1,0:T(8,128)(2,1)S(1)}, u32[]{:S(2)}, u32[]{:S(2)}) collective-permute-start(bf16[240,384]{1,0:T(8,128)(2,1)S(1)} %get-tuple-element.35.refs_4_), channel_id=1, source_target_pairs={{0,4},{2,6},{4,0},{6,2},{8,12},{10,14},{12,8},{14,10},{16,20},{18,... | collective-permute-start | bytes 552968 | tf_op jit(solution)/shard_map/apply/ppermute | solution.py:314
  25.8 6.0 %collective-permute-start.9 = (bf16[240,384]{1,0:T(8,128)(2,1)S(1)}, bf16[240,384]{1,0:T(8,128)(2,1)S(1)}, u32[]{:S(2)}, u32[]{:S(2)}) collective-permute-start(bf16[240,384]{1,0:T(8,128)(2,1)S(1)} %get-tuple-element.35.refs_4_), channel_id=1, source_target_pairs={{0,2},{2,0},{4,6},{6,4},{8,10},{10,8},{12,14},{14,12},{16,18},{18,... | collective-permute-start | bytes 552968 | tf_op jit(solution)/shard_map/apply/ppermute | solution.py:314
  28.4 3.4 %collective-permute-start.10 = (bf16[240,384]{1,0:T(8,128)(2,1)S(1)}, bf16[240,384]{1,0:T(8,128)(2,1)S(1)}, u32[]{:S(2)}, u32[]{:S(2)}) collective-permute-start(bf16[240,384]{1,0:T(8,128)(2,1)S(1)} %get-tuple-element.35.refs_4_), channel_id=1, source_target_pairs={{0,1},{1,0},{2,3},{3,2},{4,5},{5,4},{6,7},{7,6},{8,9},{9,8},{10,11... | collective-permute-start | bytes 552968 | tf_op jit(solution)/shard_map/apply/ppermute | solution.py:324
  32.5 8.5 %collective-permute-start.11 = (bf16[112,384]{1,0:T(8,128)(2,1)S(1)}, bf16[112,384]{1,0:T(8,128)(2,1)S(1)}, u32[]{:S(2)}, u32[]{:S(2)}) collective-permute-start(bf16[112,384]{1,0:T(8,128)(2,1)S(1)} %get-tuple-element.42), channel_id=1, source_target_pairs={{0,28},{2,30},{4,8},{6,10},{8,4},{10,6},{12,16},{14,18},{16,12},{1... | collective-permute-start | bytes 258056 | tf_op jit(solution)/shard_map/apply/ppermute | solution.py:314
  34.8 8.6 %collective-permute-start.12 = (bf16[112,384]{1,0:T(8,128)(2,1)S(1)}, bf16[112,384]{1,0:T(8,128)(2,1)S(1)}, u32[]{:S(2)}, u32[]{:S(2)}) collective-permute-start(bf16[112,384]{1,0:T(8,128)(2,1)S(1)} %get-tuple-element.43), channel_id=1, source_target_pairs={{0,30},{2,4},{4,2},{6,8},{8,6},{10,12},{12,10},{14,16},{16,14},{18... | collective-permute-start | bytes 258056 | tf_op jit(solution)/shard_map/apply/ppermute | solution.py:314
  37.3 8.2 %collective-permute-start.13 = (bf16[112,384]{1,0:T(8,128)(2,1)S(1)}, bf16[112,384]{1,0:T(8,128)(2,1)S(1)}, u32[]{:S(2)}, u32[]{:S(2)}) collective-permute-start(bf16[112,384]{1,0:T(8,128)(2,1)S(1)} %get-tuple-element.44), channel_id=1, source_target_pairs={{0,14},{2,16},{4,18},{6,20},{8,22},{10,24},{12,26},{14,28},{16,30}... | collective-permute-start | bytes 258056 | tf_op jit(solution)/shard_map/apply/ppermute | solution.py:314
  37.3 8.2 %collective-permute-start.14 = (bf16[112,384]{1,0:T(8,128)(2,1)S(1)}, bf16[112,384]{1,0:T(8,128)(2,1)S(1)}, u32[]{:S(2)}, u32[]{:S(2)}) collective-permute-start(bf16[112,384]{1,0:T(8,128)(2,1)S(1)} %get-tuple-element.45), channel_id=1, source_target_pairs={{0,16},{2,18},{4,20},{6,22},{8,24},{10,26},{12,28},{14,30},{16,0},... | collective-permute-start | bytes 258056 | tf_op jit(solution)/shard_map/apply/ppermute | solution.py:314
  40.9 4.9 %collective-permute-start.15 = (bf16[112,384]{1,0:T(8,128)(2,1)S(1)}, bf16[112,384]{1,0:T(8,128)(2,1)S(1)}, u32[]{:S(2)}, u32[]{:S(2)}) collective-permute-start(bf16[112,384]{1,0:T(8,128)(2,1)S(1)} %get-tuple-element.46), channel_id=1, source_target_pairs={{0,4},{2,6},{4,0},{6,2},{8,12},{10,14},{12,8},{14,10},{16,20},{18,... | collective-permute-start | bytes 258056 | tf_op jit(solution)/shard_map/apply/ppermute | solution.py:314
  41.0 5.0 %collective-permute-start.16 = (bf16[112,384]{1,0:T(8,128)(2,1)S(1)}, bf16[112,384]{1,0:T(8,128)(2,1)S(1)}, u32[]{:S(2)}, u32[]{:S(2)}) collective-permute-start(bf16[112,384]{1,0:T(8,128)(2,1)S(1)} %get-tuple-element.47), channel_id=1, source_target_pairs={{0,2},{2,0},{4,6},{6,4},{8,10},{10,8},{12,14},{14,12},{16,18},{18,... | collective-permute-start | bytes 258056 | tf_op jit(solution)/shard_map/apply/ppermute | solution.py:314
  43.4 2.6 %collective-permute-start.17 = (bf16[112,384]{1,0:T(8,128)(2,1)S(1)}, bf16[112,384]{1,0:T(8,128)(2,1)S(1)}, u32[]{:S(2)}, u32[]{:S(2)}) collective-permute-start(bf16[112,384]{1,0:T(8,128)(2,1)S(1)} %get-tuple-element.48), channel_id=1, source_target_pairs={{0,1},{1,0},{2,3},{3,2},{4,5},{5,4},{6,7},{7,6},{8,9},{9,8},{10,11... | collective-permute-start | bytes 258056 | tf_op jit(solution)/shard_map/apply/ppermute | solution.py:324
  46.4 9.1 %collective-permute-start.18 = (bf16[112,384]{1,0:T(8,128)(2,1)S(1)}, bf16[112,384]{1,0:T(8,128)(2,1)S(1)}, u32[]{:S(2)}, u32[]{:S(2)}) collective-permute-start(bf16[112,384]{1,0:T(8,128)(2,1)S(1)} %get-tuple-element.51), channel_id=1, source_target_pairs={{0,28},{2,30},{4,8},{6,10},{8,4},{10,6},{12,16},{14,18},{16,12},{1... | collective-permute-start | bytes 258056 | tf_op jit(solution)/shard_map/apply/ppermute | solution.py:314
  49.3 9.0 %collective-permute-start.19 = (bf16[112,384]{1,0:T(8,128)(2,1)S(1)}, bf16[112,384]{1,0:T(8,128)(2,1)S(1)}, u32[]{:S(2)}, u32[]{:S(2)}) collective-permute-start(bf16[112,384]{1,0:T(8,128)(2,1)S(1)} %get-tuple-element.52), channel_id=1, source_target_pairs={{0,30},{2,4},{4,2},{6,8},{8,6},{10,12},{12,10},{14,16},{16,14},{18... | collective-permute-start | bytes 258056 | tf_op jit(solution)/shard_map/apply/ppermute | solution.py:314
  52.5 7.8 %collective-permute-start.20 = (bf16[112,384]{1,0:T(8,128)(2,1)S(1)}, bf16[112,384]{1,0:T(8,128)(2,1)S(1)}, u32[]{:S(2)}, u32[]{:S(2)}) collective-permute-start(bf16[112,384]{1,0:T(8,128)(2,1)S(1)} %get-tuple-element.53), channel_id=1, source_target_pairs={{0,14},{2,16},{4,18},{6,20},{8,22},{10,24},{12,26},{14,28},{16,30}... | collective-permute-start | bytes 258056 | tf_op jit(solution)/shard_map/apply/ppermute | solution.py:314
  52.7 7.6 %collective-permute-start.21 = (bf16[112,384]{1,0:T(8,128)(2,1)S(1)}, bf16[112,384]{1,0:T(8,128)(2,1)S(1)}, u32[]{:S(2)}, u32[]{:S(2)}) collective-permute-start(bf16[112,384]{1,0:T(8,128)(2,1)S(1)} %get-tuple-element.54), channel_id=1, source_target_pairs={{0,16},{2,18},{4,20},{6,22},{8,24},{10,26},{12,28},{14,30},{16,0},... | collective-permute-start | bytes 258056 | tf_op jit(solution)/shard_map/apply/ppermute | solution.py:314
  55.5 5.2 %collective-permute-start.22 = (bf16[112,384]{1,0:T(8,128)(2,1)S(1)}, bf16[112,384]{1,0:T(8,128)(2,1)S(1)}, u32[]{:S(2)}, u32[]{:S(2)}) collective-permute-start(bf16[112,384]{1,0:T(8,128)(2,1)S(1)} %get-tuple-element.55), channel_id=1, source_target_pairs={{0,4},{2,6},{4,0},{6,2},{8,12},{10,14},{12,8},{14,10},{16,20},{18,... | collective-permute-start | bytes 258056 | tf_op jit(solution)/shard_map/apply/ppermute | solution.py:314
  55.5 5.2 %collective-permute-start.23 = (bf16[112,384]{1,0:T(8,128)(2,1)S(1)}, bf16[112,384]{1,0:T(8,128)(2,1)S(1)}, u32[]{:S(2)}, u32[]{:S(2)}) collective-permute-start(bf16[112,384]{1,0:T(8,128)(2,1)S(1)} %get-tuple-element.56), channel_id=1, source_target_pairs={{0,2},{2,0},{4,6},{6,4},{8,10},{10,8},{12,14},{14,12},{16,18},{18,... | collective-permute-start | bytes 258056 | tf_op jit(solution)/shard_map/apply/ppermute | solution.py:314
  (6 other events, 77.7 us)
